TPU v7x, 32 devices: a whole 2x2x4 slice. The times are simulated.
32 devices in a mesh: dp: 16 (over z, y, core), ctx: 2 (over x).
Axes of the slice: x: 2, y: 2, z: 4, core: 2. Of those that a mesh axis runs over, the one named last changes fastest.
Arguments:
- frames: bfloat16 [16, 1024, 1280], P('dp', 'ctx'), may hold values from -6 to 6
- conv_taps: float32 [31, 1280], replicated, may hold values from -1 to 1
- conv_gain: float32 [1280], replicated, may hold values from 0.1 to 1.9
- w_kv: bfloat16 [1280, 2560], P('dp'), may hold values from -0.15625 to 0.15625
- queries: bfloat16 [16, 32, 1280], P('dp', 'ctx'), may hold values from -6 to 6
- out_grad: bfloat16 [16, 32, 1280], P('dp', 'ctx'), may hold values from -6 to 6
- frame_len: int32 [16], P('dp'), may hold values from 256 to 1024
- token_len: int32 [16], P('dp'), may hold values from 8 to 32
Outputs:
- frames_grad: bfloat16 [16, 1024, 1280], P('dp', 'ctx')
- taps_grad: float32 [31, 1280], replicated
- gain_grad: float32 [1280], replicated
- w_kv_grad: float32 [1280, 2560], P('dp')
- queries_grad: bfloat16 [16, 32, 1280], P('dp', 'ctx')
Inputs may be any that keep to these rules, and one draw needn't show every extreme that they name: frames at positions of frame_len[b] or beyond are padding of utterance b. Tokens at positions of token_len[b] or beyond are padding of utterance b.
All inputs are finite; a program needn't handle non-finite values.
Results may differ from a plain program's by a relative error of at most 0.012.
Values may be sent and summed in bfloat16 or wider, within the bound.
A program may use at most 128 MiB of HBM per device.

v0:
```python
import jax
import jax.numpy as jnp
from jax import lax
from jax.sharding import PartitionSpec as P

HEADS = 20


def padded_2(block, sides, width):
    for axis, dim in sides:
        count = lax.axis_size(axis)
        forward = [(i, i + 1) for i in range(count - 1)]
        backward = [(target, source) for source, target in forward]
        low = lax.ppermute(
            lax.slice_in_dim(block, block.shape[dim] - width, None, axis=dim), axis, forward
        )
        high = lax.ppermute(lax.slice_in_dim(block, 0, width, axis=dim), axis, backward)
        block = jnp.concatenate([low, block, high], axis=dim)
    return block


def shifted(value, axis, steps):
    count = lax.axis_size(axis)
    pairs = [(source, (source + steps) % count) for source in range(count)]
    return lax.ppermute(value, axis, pairs)


def conv_time(padded, conv_taps, length):
    total = jnp.zeros((length, padded.shape[1]), jnp.float32)
    for tap_idx in range(conv_taps.shape[0]):
        total = total + conv_taps[tap_idx] * padded[tap_idx : tap_idx + length].astype(jnp.float32)
    return total


def silu_slope(gated):
    sigma = jax.nn.sigmoid(gated)
    return sigma * (1.0 + gated * (1.0 - sigma))


def forward_part(query_block, key_block, value_block, live_mask, head_count):
    row_count = query_block.shape[0]
    frame_count = key_block.shape[0]
    q_heads = query_block.reshape(row_count, head_count, -1)
    k_heads = key_block.reshape(frame_count, head_count, -1)
    v_heads = value_block.reshape(frame_count, head_count, -1)
    scale = q_heads.shape[2] ** (-0.5)
    exp_scores = (
        jnp.exp(
            jnp.einsum("thd,fhd->htf", q_heads, k_heads, preferred_element_type=jnp.float32) * scale
        )
        * live_mask
    )
    totals = jnp.sum(exp_scores, axis=2).T
    weighted = jnp.einsum(
        "htf,fhd->thd", exp_scores.astype(jnp.bfloat16), v_heads, preferred_element_type=jnp.float32
    )
    return (weighted.reshape(row_count, -1), totals)


def backward_part(
    query_block, grad_block, totals, delta_rows, key_block, value_block, live_mask, head_count
):
    row_count = query_block.shape[0]
    frame_count = key_block.shape[0]
    q_heads = query_block.reshape(row_count, head_count, -1)
    g_heads = grad_block.reshape(row_count, head_count, -1)
    k_heads = key_block.reshape(frame_count, head_count, -1)
    v_heads = value_block.reshape(frame_count, head_count, -1)
    scale = q_heads.shape[2] ** (-0.5)
    exp_scores = (
        jnp.exp(
            jnp.einsum("thd,fhd->htf", q_heads, k_heads, preferred_element_type=jnp.float32) * scale
        )
        * live_mask
    )
    attn_prob = exp_scores / totals.T[:, :, None]
    d_prob = jnp.einsum("thd,fhd->htf", g_heads, v_heads, preferred_element_type=jnp.float32)
    d_score = (attn_prob * (d_prob - delta_rows.T[:, :, None])).astype(jnp.bfloat16)
    query_part = jnp.einsum(
        "htf,fhd->thd", d_score, k_heads, preferred_element_type=jnp.float32
    ).reshape(row_count, -1)
    key_part = jnp.einsum(
        "htf,thd->fhd", d_score, q_heads, preferred_element_type=jnp.float32
    ).reshape(frame_count, -1)
    value_part = jnp.einsum(
        "htf,thd->fhd", attn_prob.astype(jnp.bfloat16), g_heads, preferred_element_type=jnp.float32
    ).reshape(frame_count, -1)
    return (query_part, key_part, value_part)


def row_delta(weighted, totals, grad_block):
    row_count = weighted.shape[0]
    head_count = totals.shape[1]
    head_dim = weighted.shape[1] // head_count
    attended = weighted / jnp.repeat(totals, head_dim, axis=1)
    return jnp.sum(
        (grad_block.astype(jnp.float32) * attended).reshape(row_count, head_count, head_dim), axis=2
    )


def per_device(frames, conv_taps, conv_gain, w_kv, queries, out_grad, frame_len, token_len):
    cycle_size = lax.axis_size("ctx")
    cycle_pos = lax.axis_index("ctx")
    length = frames.shape[1]
    model_width = frames.shape[2]
    tokens = queries.shape[1]
    tap_count = conv_taps.shape[0]
    rim_width = tap_count // 2
    scale = (model_width // HEADS) ** (-0.5)
    padded = padded_2(frames, (("ctx", 1),), rim_width)[0]
    conv_out = conv_time(padded, conv_taps, length)
    gated = conv_gain * conv_out
    encoded = (frames[0].astype(jnp.float32) + jax.nn.silu(gated)).astype(jnp.bfloat16)
    w_full = lax.all_gather(w_kv, "dp", axis=0, tiled=True)
    key_values = jnp.dot(encoded, w_full, preferred_element_type=jnp.float32).astype(jnp.bfloat16)
    key_block = key_values[:, :model_width]
    value_block = key_values[:, model_width:]
    frame_pos = cycle_pos * length + jnp.arange(length)
    live_mask = (frame_pos < frame_len[0]).astype(jnp.float32)
    token_pos = cycle_pos * tokens + jnp.arange(tokens)
    grad_block = out_grad[0] * (token_pos < token_len[0]).astype(jnp.bfloat16)[:, None]
    query_block = queries[0]

    def forward_tile(visitor, keys_part, values_part, head_count):
        return forward_part(visitor, keys_part, values_part, live_mask, head_count)

    def backward_tile(
        visitor, visit_grad, visit_totals, visit_delta, keys_part, values_part, head_count
    ):
        return backward_part(
            visitor,
            visit_grad,
            visit_totals,
            visit_delta,
            keys_part,
            values_part,
            live_mask,
            head_count,
        )

    def forward_turn(turn_idx, carried):
        visitor, weighted, totals = carried
        part_sum, part_total = forward_tile(visitor, key_block, value_block, HEADS)
        visitor = shifted(visitor, "ctx", 1)
        weighted, totals = shifted((weighted + part_sum, totals + part_total), "ctx", 1)
        return (visitor, weighted, totals)

    first_state = (
        query_block,
        jnp.zeros((tokens, model_width), jnp.float32),
        jnp.zeros((tokens, HEADS), jnp.float32),
    )
    first_out = lax.fori_loop(0, cycle_size, forward_turn, first_state)
    totals = first_out[2]
    delta_rows = row_delta(first_out[1], totals, grad_block)

    def backward_turn(turn_idx, carried):
        visitor, visit_grad, visit_totals, visit_delta, query_acc, key_acc, value_acc = carried
        part_query, part_key, part_value = backward_tile(
            visitor, visit_grad, visit_totals, visit_delta, key_block, value_block, HEADS
        )
        visitor, visit_grad = shifted((visitor, visit_grad), "ctx", 1)
        visit_totals, visit_delta, query_acc = shifted(
            (visit_totals, visit_delta, query_acc + part_query), "ctx", 1
        )
        return (
            visitor,
            visit_grad,
            visit_totals,
            visit_delta,
            query_acc,
            key_acc + part_key,
            value_acc + part_value,
        )

    second_state = (
        query_block,
        grad_block,
        totals,
        delta_rows,
        jnp.zeros((tokens, model_width), jnp.float32),
        jnp.zeros((length, model_width), jnp.float32),
        jnp.zeros((length, model_width), jnp.float32),
    )
    second_out = lax.fori_loop(0, cycle_size, backward_turn, second_state)
    query_acc = second_out[4]
    key_acc = second_out[5]
    value_acc = second_out[6]
    queries_grad = (query_acc * scale).astype(jnp.bfloat16)[None]
    kv_grad = jnp.concatenate([key_acc * scale, value_acc], 1).astype(jnp.bfloat16)
    enc_grad = lax.dot_general(
        kv_grad, w_full, (((1,), (1,)), ((), ())), preferred_element_type=jnp.float32
    )
    gated_grad = enc_grad * silu_slope(gated)
    gain_term = jnp.sum(gated_grad * conv_out, axis=0)
    conv_grad = gated_grad * conv_gain
    tap_terms = jnp.stack(
        [
            jnp.sum(conv_grad * padded[tap_idx : tap_idx + length].astype(jnp.float32), axis=0)
            for tap_idx in range(tap_count)
        ]
    )
    padded_grad = padded_2(conv_grad[None], (("ctx", 1),), rim_width)[0]
    back_conv = jnp.zeros((length, model_width), jnp.float32)
    for tap_idx in range(tap_count):
        offset = 2 * rim_width - tap_idx
        back_conv = back_conv + conv_taps[tap_idx] * padded_grad[offset : offset + length]
    frames_grad = (enc_grad + back_conv).astype(jnp.bfloat16)[None]
    taps_grad, gain_grad = lax.psum((tap_terms, gain_term), ("dp", "ctx"))
    data_part = lax.psum_scatter(
        lax.dot_general(
            encoded, kv_grad, (((0,), (0,)), ((), ())), preferred_element_type=jnp.float32
        ),
        "dp",
        scatter_dimension=0,
        tiled=True,
    )
    w_kv_grad = lax.psum(data_part, "ctx")
    return (frames_grad, taps_grad, gain_grad, w_kv_grad, queries_grad)


def solution(mesh):
    placed = (
        P("dp", "ctx", None),
        P(),
        P(),
        P("dp", None),
        P("dp", "ctx", None),
        P("dp", "ctx", None),
        P("dp"),
        P("dp"),
    )
    return jax.shard_map(
        per_device,
        mesh=mesh,
        in_specs=placed,
        out_specs=(P("dp", "ctx", None), P(), P(), P("dp", None), P("dp", "ctx", None)),
        check_vma=False,
    )
```

profile of v0, /device:TPU:0, one launch (start us, length us, event | category | flops | bytes accessed | tf_op | source)
XLA Modules:
  0.0 496.1 jit_solution(5663490250576671858)
XLA Ops:
  7.2 1.5 copy.116
  8.8 0.8 fusion.243
  9.6 4.8 collective-permute-start.8
  14.5 1.3 collective-permute-start.9
  16.4 1.5 slice_reduce_fusion.29
  18.0 1.8 slice_reduce_fusion.30
  19.9 1.5 constant_dynamic-update-slice_fusion.1
  21.5 0.8 copy.76
  22.3 12.4 %fusion.82 = (bf16[512,1280]{1,0:T(8,128)(2,1)}, f32[512,1280]{1,0:T(8,128)}) fusion(bf16[1,512,1280]{2,1,0:T(8,128)(2,1)S(1)} %copy-done.4, f32[1280]{0:T(1024)S(1)} %copy-done.75, bf16[1,527,1280]{2,1,0:T(8,128)(2,1)S(1)} %constant_dynamic-update-slice_fusion, f32[1280]{0:T(1024)S(1)} %get-tuple-element.290, f32[1280]{0:T(1024)S(1)} %get-tuple-element.291, ...), kind=kLoop, calls=%fused_computation.196 | loop fusion | flops 104202240 | bytes 25105920 | tf_op jit(solution)/shard_map/convert_element_type | solution.py:113
  35.0 41.4 %all-gather.2.cloned.1.call-done = bf16[1280,2560]{1,0:T(8,128)(2,1)} async-done(((bf16[80,2560]{1,0:T(8,128)(2,1)}), bf16[1280,2560]{1,0:T(8,128)(2,1)}) %all-gather.2.cloned.1.call-update) | async-done | bytes 6553616 | tf_op jit(solution)/shard_map/all_gather | solution.py:114
  76.4 6.8 %convolution_convert_fusion = bf16[512,2560]{1,0:T(8,128)(2,1)S(1)} fusion(bf16[512,1280]{1,0:T(8,128)(2,1)} %get-tuple-element.335, bf16[1280,2560]{1,0:T(8,128)(2,1)} %all-gather.2.cloned.1.call-done), kind=kOutput, calls=%fused_computation.72 | convolution fusion | flops 3356753920 | bytes 10485760 | tf_op jit(solution)/shard_map/dot_general | solution.py:115
  83.3 1.7 fusion.242
  85.0 1.6 copy.43
  86.6 2.4 copy.42
  89.6 19.6 %while.38 = (s32[]{:T(128)}, bf16[16,1280]{1,0:T(8,128)(2,1)S(1)}, f32[16,1280]{1,0:T(8,128)S(1)}, f32[16,20]{0,1:T(8,128)}, bf16[512,1280]{0,1:T(8,128)(2,1)}, ...) while((s32[]{:T(128)}, bf16[16,1280]{1,0:T(8,128)(2,1)S(1)}, ...), condition=%wide.region_2.3_spmd.clone, body=%wide.region_0.2_spmd.clone.sunk | while | flops 42620416 | bytes 4643037 | solution.py:153
  89.7 1.5 collective-permute-start
  92.0 1.7 fusion.280
  95.7 1.5 collective-permute-start.2
  97.1 2.3 collective-permute-done.2
  99.5 1.5 collective-permute-start
  101.8 1.7 fusion.280
  105.5 1.5 collective-permute-start.2
  106.9 2.3 collective-permute-done.2
  112.5 56.3 %while.39 = (s32[]{:T(128)}, bf16[16,1280]{1,0:T(8,128)(2,1)}, bf16[16,1280]{1,0:T(8,128)(2,1)}, f32[16,20]{0,1:T(8,128)}, f32[16,20]{0,1:T(8,128)}, /*index=5*/...) while((s32[]{:T(128)}, bf16[16,1280]{1,0:T(8,128)(2,1)}, ...), condition=%wide.region_5.6_spmd.clone, body=%wide.region_4.5_spmd.clone.sunk | while | flops 108647936 | bytes 37869488 | solution.py:185
  112.5 1.3 copy.98
  113.8 1.5 collective-permute-start.5
  115.3 1.3 copy.99
  117.9 1.5 collective-permute-start.3
  121.6 1.7 fusion.292
  123.4 0.8 copy-done.3
  124.2 1.0 fusion.293
  125.8 0.9 add.1597
  126.7 1.5 collective-permute-start.7
  128.3 3.1 fusion.294
  131.4 2.1 fusion.295
  133.5 6.1 %bitcast_add_fusion.6 = (f32[512,1280]{0,1:T(8,128)}, f32[512,1280]{0,1:T(8,128)}) fusion(f32[20,512,64]{1,2,0:T(8,128)} %fusion.294, f32[512,1280]{0,1:T(8,128)} %get-tuple-element.528, pred[]{:T(512)S(6)} %compare.3, f32[20,512,64]{1,2,0:T(8,128)} %fusion.295, f32[512,1280]{0,1:T(8,128)} %get-tuple-element.527), kind=kLoop, calls=%fused_computation.11.clone.1 | loop fusion | flops 2621440 | bytes 15728641 | tf_op jit(solution)/shard_map/while/body/eval_jaxpr/add | solution.py:173
  140.3 1.3 copy.98
  142.2 1.3 copy.99
  143.5 1.5 collective-permute-start.6
  147.1 1.5 collective-permute-start.4
  149.5 1.7 fusion.292
  151.2 0.8 copy-done.3
  152.1 1.0 fusion.293
  153.7 0.9 add.1597
  155.2 3.1 fusion.294
  158.4 2.1 fusion.295
  160.5 7.7 %bitcast_add_fusion.6 = (f32[512,1280]{0,1:T(8,128)}, f32[512,1280]{0,1:T(8,128)}) fusion(f32[20,512,64]{1,2,0:T(8,128)} %fusion.294, f32[512,1280]{0,1:T(8,128)} %get-tuple-element.528, pred[]{:T(512)S(6)} %compare.3, f32[20,512,64]{1,2,0:T(8,128)} %fusion.295, f32[512,1280]{0,1:T(8,128)} %get-tuple-element.527), kind=kLoop, calls=%fused_computation.11.clone.1 | loop fusion | flops 2621440 | bytes 15728641 | tf_op jit(solution)/shard_map/while/body/eval_jaxpr/add | solution.py:173
  168.8 2.2 multiply_convert_fusion
  171.5 1.1 copy-done.11
  172.6 7.7 %fusion.204 = f32[1280,2560]{1,0:T(8,128)} fusion(bf16[512,1280]{1,0:T(8,128)(2,1)S(1)} %copy-done.10, bf16[512,1280]{0,1:T(8,128)(2,1)S(1)} %convert.38, bf16[512,1280]{0,1:T(8,128)(2,1)S(1)} %multiply_convert_fusion), kind=kOutput, calls=%fused_computation.348 | convolution fusion | flops 3360686080 | bytes 17039360 | tf_op jit(solution)/shard_map/dot_general | solution.py:211
  180.6 7.0 %fusion.205 = f32[512,1280]{1,0:T(8,128)S(1)} fusion(bf16[1280,2560]{1,0:T(8,128)(2,1)} %all-gather.2.cloned.1.call-done, bf16[512,1280]{0,1:T(8,128)(2,1)} %copy-done.11, bf16[512,1280]{0,1:T(8,128)(2,1)S(1)} %multiply_convert_fusion), kind=kOutput, calls=%fused_computation.349 | convolution fusion | flops 3360686080 | bytes 11796480 | tf_op jit(solution)/shard_map/dot_general | solution.py:191
  187.7 6.7 %fusion.81 = (f32[1280]{0:T(1024)S(1)}, f32[1280]{0:T(1024)S(1)}, f32[1280]{0:T(1024)S(1)}, f32[1280]{0:T(1024)S(1)}, f32[1280]{0:T(1024)S(1)}, /*index=5*/f32[1...) fusion(bf16[1,527,1280]{2,1,0:T(8,128)(2,1)S(1)} %constant_dyna, ...), kind=kLoop, calls=%fused_computation.195 | loop fusion | flops 37335040 | bytes 27612160 | tf_op jit(solution)/shard_map/reduce_sum | solution.py:199
  194.6 2.6 fusion.52
  197.6 3.3 fusion.61
  201.0 1.3 collective-permute-start.10
  202.3 4.6 collective-permute-start.11
  206.9 2.7 stack.127
  210.3 44.2 %psum.22 = f32[1280]{0:T(1024)} all-reduce(f32[1280]{0:T(1024)S(1)} %get-tuple-element.341), channel_id=1, replica_groups=mesh['dp'=16,'ctx'=2] {'dp','ctx'}, use_global_device_ids=true, to_apply=%region_39.40 | all-reduce | flops 1280 | bytes 10240 | tf_op jit(solution)/shard_map/psum | solution.py:209
  254.5 64.0 %reduce-scatter.2.cloned.1.call-done = f32[80,2560]{1,0:T(8,128)} async-done(((f32[1280,2560]{1,0:T(8,128)}), f32[80,2560]{1,0:T(8,128)}) %reduce-scatter.2.cloned.1.call-update) | async-done | bytes 819216 | tf_op jit(solution)/shard_map/reduce_scatter | solution.py:210
  318.8 43.9 %fusion.235 = bf16[1,512,1280]{2,1,0:T(8,128)(2,1)} fusion(f32[512,1280]{1,0:T(8,128)} %copy-done.6, f32[1,512,1280]{2,1,0:T(8,128)} %bitcast.634, f32[1,15,1280]{2,1,0:T(8,128)S(1)} %collective-permute-done.11, f32[1280]{0:T(1024)S(1)} %copy-done.33, f32[1280]{0:T(1024)S(1)} %copy-done.35, f32[1280]{0:T(1024)S(1)} %copy-done.39, f32[1280]{0:T(1024)S(1)} %copy-done.41, ...), kind=kLoop, calls=%fused_computation.396 | loop fusion | flops 60948480 | bytes 9487360 | tf_op jit(solution)/shard_map/broadcast_in_dim | solution.py:208
  362.7 83.9 %all-reduce.3.cloned.1.call-done = f32[31,1280]{1,0:T(8,128)} async-done(((f32[31,1280]{1,0:T(8,128)}), f32[31,1280]{1,0:T(8,128)}) %all-reduce.3.cloned.1.call-update) | async-done | bytes 158736 | tf_op jit(solution)/shard_map/psum | solution.py:209
  446.5 39.3 %all-reduce.5.cloned.1.call-done = f32[80,2560]{1,0:T(8,128)} async-done(((f32[80,2560]{1,0:T(8,128)}), f32[80,2560]{1,0:T(8,128)}) %all-reduce.5.cloned.1.call-update) | async-done | bytes 819216 | tf_op jit(solution)/shard_map/psum | solution.py:218
  485.9 1.6 copy.117
  487.5 2.1 copy.118
  (270 shorter events, 21.6 us)
Async XLA Ops:
  7.2 69.2 %all-gather.2.cloned.1.call-start = ((), (), s32[]{:S(2)}) async-start(), calls=%async_computation.1 | async-start | bytes 6963200 | tf_op jit(solution)/shard_map/all_gather | solution.py:114
  8.7 309.7 %reduce-scatter.2.cloned.1.call-start = ((), (), s32[]{:S(2)}) async-start(), calls=%async_computation.3 | async-start | bytes 13926400 | tf_op jit(solution)/shard_map/reduce_scatter | solution.py:210
  9.6 12.7 %collective-permute-start.8 = (bf16[1,15,1280]{2,1,0:T(8,128)(2,1)S(1)}, bf16[1,15,1280]{2,1,0:T(8,128)(2,1)S(1)}, u32[]{:S(2)}, u32[]{:S(2)}) collective-permute-start(bf16[1,15,1280]{2,1,0:T(8,128)(2,1)S(1)} %get-tuple-element.346), channel_id=1, source_target_pairs={{0,1},{2,3},{4,5},{6,7},{8,9},{10,11},{12,13},{14,15},{16,17},{18,... | collective-permute-start | bytes 115208 | tf_op jit(solution)/shard_map/ppermute | solution.py:14
  14.5 7.8 %collective-permute-start.9 = (bf16[1,15,1280]{2,1,0:T(8,128)(2,1)S(1)}, bf16[1,15,1280]{2,1,0:T(8,128)(2,1)S(1)}, u32[]{:S(2)}, u32[]{:S(2)}) collective-permute-start(bf16[1,15,1280]{2,1,0:T(8,128)(2,1)S(1)} %get-tuple-element.347), channel_id=1, source_target_pairs={{1,0},{3,2},{5,4},{7,6},{9,8},{11,10},{13,12},{15,14},{17,16},{19,... | collective-permute-start | bytes 115208 | tf_op jit(solution)/shard_map/ppermute | solution.py:17
  17.9 16.8 %copy-start.14 = (f32[1280]{0:T(1024)}, f32[1280]{0:T(1024)S(1)}, u32[]{:S(2)}) copy-start(f32[1280]{0:T(1024)S(1)} %get-tuple-element.281) | copy-start | bytes 15364
  17.9 16.8 %copy-start.16 = (f32[1280]{0:T(1024)}, f32[1280]{0:T(1024)S(1)}, u32[]{:S(2)}) copy-start(f32[1280]{0:T(1024)S(1)} %get-tuple-element.282) | copy-start | bytes 15364
  17.9 16.8 %copy-start.18 = (f32[1280]{0:T(1024)}, f32[1280]{0:T(1024)S(1)}, u32[]{:S(2)}) copy-start(f32[1280]{0:T(1024)S(1)} %get-tuple-element.283) | copy-start | bytes 15364
  17.9 16.8 %copy-start.20 = (f32[1280]{0:T(1024)}, f32[1280]{0:T(1024)S(1)}, u32[]{:S(2)}) copy-start(f32[1280]{0:T(1024)S(1)} %get-tuple-element.284) | copy-start | bytes 15364
  17.9 16.8 %copy-start.22 = (f32[1280]{0:T(1024)}, f32[1280]{0:T(1024)S(1)}, u32[]{:S(2)}) copy-start(f32[1280]{0:T(1024)S(1)} %get-tuple-element.285) | copy-start | bytes 15364
  17.9 16.8 %copy-start.24 = (f32[1280]{0:T(1024)}, f32[1280]{0:T(1024)S(1)}, u32[]{:S(2)}) copy-start(f32[1280]{0:T(1024)S(1)} %get-tuple-element.286) | copy-start | bytes 15364
  17.9 16.8 %copy-start.26 = (f32[1280]{0:T(1024)}, f32[1280]{0:T(1024)S(1)}, u32[]{:S(2)}) copy-start(f32[1280]{0:T(1024)S(1)} %get-tuple-element.287) | copy-start | bytes 15364
  17.9 16.8 %copy-start.28 = (f32[1280]{0:T(1024)}, f32[1280]{0:T(1024)S(1)}, u32[]{:S(2)}) copy-start(f32[1280]{0:T(1024)S(1)} %get-tuple-element.288) | copy-start | bytes 15364
  18.0 16.8 %copy-start.30 = (f32[1280]{0:T(1024)}, f32[1280]{0:T(1024)S(1)}, u32[]{:S(2)}) copy-start(f32[1280]{0:T(1024)S(1)} %get-tuple-element.289) | copy-start | bytes 15364
  89.6 20.6 %copy-start.74 = (bf16[1,16,1280]{2,1,0:T(8,128)(2,1)S(1)}, bf16[1,16,1280]{2,1,0:T(8,128)(2,1)}, u32[]{:S(2)}) copy-start(bf16[1,16,1280]{2,1,0:T(8,128)(2,1)} %param.17) | copy-start | bytes 122884
  89.7 9.8 %collective-permute-start = (bf16[16,1280]{1,0:T(8,128)(2,1)S(1)}, bf16[16,1280]{1,0:T(8,128)(2,1)S(1)}, u32[]{:S(2)}, u32[]{:S(2)}) collective-permute-start(bf16[16,1280]{1,0:T(8,128)(2,1)S(1)} %copy.80), channel_id=1, source_target_pairs={{0,1},{1,0},{2,3},{3,2},{4,5},{5,4},{6,7},{7,6},{8,9},{9,8},{10,11... | collective-permute-start | bytes 122888 | tf_op jit(solution)/shard_map/while/body/eval_jaxpr/ppermute | solution.py:25
  94.3 5.1 %collective-permute-start.1 = (f32[16,1280]{1,0:T(8,128)S(1)}, f32[16,1280]{1,0:T(8,128)S(1)}, u32[]{:S(2)}, u32[]{:S(2)}) collective-permute-start(f32[16,1280]{1,0:T(8,128)S(1)} %add.1592), channel_id=1, source_target_pairs={{0,1},{1,0},{2,3},{3,2},{4,5},{5,4},{6,7},{7,6},{8,9},{9,8},{10,11... | collective-permute-start | bytes 245768 | tf_op jit(solution)/shard_map/while/body/eval_jaxpr/ppermute | solution.py:25
  95.7 3.8 collective-permute-start.2
  99.5 9.8 %collective-permute-start = (bf16[16,1280]{1,0:T(8,128)(2,1)S(1)}, bf16[16,1280]{1,0:T(8,128)(2,1)S(1)}, u32[]{:S(2)}, u32[]{:S(2)}) collective-permute-start(bf16[16,1280]{1,0:T(8,128)(2,1)S(1)} %copy.80), channel_id=1, source_target_pairs={{0,1},{1,0},{2,3},{3,2},{4,5},{5,4},{6,7},{7,6},{8,9},{9,8},{10,11... | collective-permute-start | bytes 122888 | tf_op jit(solution)/shard_map/while/body/eval_jaxpr/ppermute | solution.py:25
  104.1 5.1 %collective-permute-start.1 = (f32[16,1280]{1,0:T(8,128)S(1)}, f32[16,1280]{1,0:T(8,128)S(1)}, u32[]{:S(2)}, u32[]{:S(2)}) collective-permute-start(f32[16,1280]{1,0:T(8,128)S(1)} %add.1592), channel_id=1, source_target_pairs={{0,1},{1,0},{2,3},{3,2},{4,5},{5,4},{6,7},{7,6},{8,9},{9,8},{10,11... | collective-permute-start | bytes 245768 | tf_op jit(solution)/shard_map/while/body/eval_jaxpr/ppermute | solution.py:25
  105.5 3.8 collective-permute-start.2
  113.8 25.9 %collective-permute-start.5 = (f32[16,20]{0,1:T(8,128)}, f32[16,20]{0,1:T(8,128)}, u32[]{:S(2)}, u32[]{:S(2)}) collective-permute-start(f32[16,20]{0,1:T(8,128)} %copy.98), channel_id=1, source_target_pairs={{0,1},{1,0},{2,3},{3,2},{4,5},{5,4},{6,7},{7,6},{8,9},{9,8},{10,11... | collective-permute-start | bytes 3848 | tf_op jit(solution)/shard_map/while/body/eval_jaxpr/ppermute | solution.py:25
  116.6 23.1 %collective-permute-start.6 = (f32[16,20]{0,1:T(8,128)}, f32[16,20]{0,1:T(8,128)}, u32[]{:S(2)}, u32[]{:S(2)}) collective-permute-start(f32[16,20]{0,1:T(8,128)} %copy.99), channel_id=1, source_target_pairs={{0,1},{1,0},{2,3},{3,2},{4,5},{5,4},{6,7},{7,6},{8,9},{9,8},{10,11... | collective-permute-start | bytes 3848 | tf_op jit(solution)/shard_map/while/body/eval_jaxpr/ppermute | solution.py:25
  117.9 21.8 %collective-permute-start.3 = (bf16[16,1280]{1,0:T(8,128)(2,1)S(1)}, bf16[16,1280]{1,0:T(8,128)(2,1)}, u32[]{:S(2)}, u32[]{:S(2)}) collective-permute-start(bf16[16,1280]{1,0:T(8,128)(2,1)S(1)} %copy.96), channel_id=1, source_target_pairs={{0,1},{1,0},{2,3},{3,2},{4,5},{5,4},{6,7},{7,6},{8,9},{9,8},{10,11... | collective-permute-start | bytes 122888 | tf_op jit(solution)/shard_map/while/body/eval_jaxpr/ppermute | solution.py:25
  120.2 19.5 %collective-permute-start.4 = (bf16[16,1280]{1,0:T(8,128)(2,1)S(1)}, bf16[16,1280]{1,0:T(8,128)(2,1)}, u32[]{:S(2)}, u32[]{:S(2)}) collective-permute-start(bf16[16,1280]{1,0:T(8,128)(2,1)S(1)} %copy.97), channel_id=1, source_target_pairs={{0,1},{1,0},{2,3},{3,2},{4,5},{5,4},{6,7},{7,6},{8,9},{9,8},{10,11... | collective-permute-start | bytes 122888 | tf_op jit(solution)/shard_map/while/body/eval_jaxpr/ppermute | solution.py:25
  126.7 13.0 %collective-permute-start.7 = (f32[16,1280]{1,0:T(8,128)S(1)}, f32[16,1280]{1,0:T(8,128)S(1)}, u32[]{:S(2)}, u32[]{:S(2)}) collective-permute-start(f32[16,1280]{1,0:T(8,128)S(1)} %add.1597), channel_id=1, source_target_pairs={{0,1},{1,0},{2,3},{3,2},{4,5},{5,4},{6,7},{7,6},{8,9},{9,8},{10,11... | collective-permute-start | bytes 245768 | tf_op jit(solution)/shard_map/while/body/eval_jaxpr/ppermute | solution.py:25
  141.7 26.5 %collective-permute-start.5 = (f32[16,20]{0,1:T(8,128)}, f32[16,20]{0,1:T(8,128)}, u32[]{:S(2)}, u32[]{:S(2)}) collective-permute-start(f32[16,20]{0,1:T(8,128)} %copy.98), channel_id=1, source_target_pairs={{0,1},{1,0},{2,3},{3,2},{4,5},{5,4},{6,7},{7,6},{8,9},{9,8},{10,11... | collective-permute-start | bytes 3848 | tf_op jit(solution)/shard_map/while/body/eval_jaxpr/ppermute | solution.py:25
  143.5 24.6 %collective-permute-start.6 = (f32[16,20]{0,1:T(8,128)}, f32[16,20]{0,1:T(8,128)}, u32[]{:S(2)}, u32[]{:S(2)}) collective-permute-start(f32[16,20]{0,1:T(8,128)} %copy.99), channel_id=1, source_target_pairs={{0,1},{1,0},{2,3},{3,2},{4,5},{5,4},{6,7},{7,6},{8,9},{9,8},{10,11... | collective-permute-start | bytes 3848 | tf_op jit(solution)/shard_map/while/body/eval_jaxpr/ppermute | solution.py:25
  145.8 22.4 %collective-permute-start.3 = (bf16[16,1280]{1,0:T(8,128)(2,1)S(1)}, bf16[16,1280]{1,0:T(8,128)(2,1)}, u32[]{:S(2)}, u32[]{:S(2)}) collective-permute-start(bf16[16,1280]{1,0:T(8,128)(2,1)S(1)} %copy.96), channel_id=1, source_target_pairs={{0,1},{1,0},{2,3},{3,2},{4,5},{5,4},{6,7},{7,6},{8,9},{9,8},{10,11... | collective-permute-start | bytes 122888 | tf_op jit(solution)/shard_map/while/body/eval_jaxpr/ppermute | solution.py:25
  147.1 21.1 %collective-permute-start.4 = (bf16[16,1280]{1,0:T(8,128)(2,1)S(1)}, bf16[16,1280]{1,0:T(8,128)(2,1)}, u32[]{:S(2)}, u32[]{:S(2)}) collective-permute-start(bf16[16,1280]{1,0:T(8,128)(2,1)S(1)} %copy.97), channel_id=1, source_target_pairs={{0,1},{1,0},{2,3},{3,2},{4,5},{5,4},{6,7},{7,6},{8,9},{9,8},{10,11... | collective-permute-start | bytes 122888 | tf_op jit(solution)/shard_map/while/body/eval_jaxpr/ppermute | solution.py:25
  154.6 13.6 %collective-permute-start.7 = (f32[16,1280]{1,0:T(8,128)S(1)}, f32[16,1280]{1,0:T(8,128)S(1)}, u32[]{:S(2)}, u32[]{:S(2)}) collective-permute-start(f32[16,1280]{1,0:T(8,128)S(1)} %add.1597), channel_id=1, source_target_pairs={{0,1},{1,0},{2,3},{3,2},{4,5},{5,4},{6,7},{7,6},{8,9},{9,8},{10,11... | collective-permute-start | bytes 245768 | tf_op jit(solution)/shard_map/while/body/eval_jaxpr/ppermute | solution.py:25
  180.4 266.2 %all-reduce.3.cloned.1.call-start = ((), (), s32[]{:S(2)}) async-start(), calls=%async_computation.2 | async-start | bytes 327680 | tf_op jit(solution)/shard_map/psum | solution.py:209
  197.3 121.2 %copy-start.15 = (f32[1280]{0:T(1024)S(1)}, f32[1280]{0:T(1024)}, u32[]{:S(2)}) copy-start(f32[1280]{0:T(1024)} %copy-done.14) | copy-start | bytes 15364
  197.3 121.2 %copy-start.17 = (f32[1280]{0:T(1024)S(1)}, f32[1280]{0:T(1024)}, u32[]{:S(2)}) copy-start(f32[1280]{0:T(1024)} %copy-done.16) | copy-start | bytes 15364
  197.3 121.2 %copy-start.19 = (f32[1280]{0:T(1024)S(1)}, f32[1280]{0:T(1024)}, u32[]{:S(2)}) copy-start(f32[1280]{0:T(1024)} %copy-done.18) | copy-start | bytes 15364
  197.3 121.2 %copy-start.21 = (f32[1280]{0:T(1024)S(1)}, f32[1280]{0:T(1024)}, u32[]{:S(2)}) copy-start(f32[1280]{0:T(1024)} %copy-done.20) | copy-start | bytes 15364
  197.3 121.2 %copy-start.23 = (f32[1280]{0:T(1024)S(1)}, f32[1280]{0:T(1024)}, u32[]{:S(2)}) copy-start(f32[1280]{0:T(1024)} %copy-done.22) | copy-start | bytes 15364
  197.3 121.2 %copy-start.25 = (f32[1280]{0:T(1024)S(1)}, f32[1280]{0:T(1024)}, u32[]{:S(2)}) copy-start(f32[1280]{0:T(1024)} %copy-done.24) | copy-start | bytes 15364
  197.3 121.2 %copy-start.27 = (f32[1280]{0:T(1024)S(1)}, f32[1280]{0:T(1024)}, u32[]{:S(2)}) copy-start(f32[1280]{0:T(1024)} %copy-done.26) | copy-start | bytes 15364
  197.4 121.2 %copy-start.29 = (f32[1280]{0:T(1024)S(1)}, f32[1280]{0:T(1024)}, u32[]{:S(2)}) copy-start(f32[1280]{0:T(1024)} %copy-done.28) | copy-start | bytes 15364
  197.4 121.2 %copy-start.31 = (f32[1280]{0:T(1024)S(1)}, f32[1280]{0:T(1024)}, u32[]{:S(2)}) copy-start(f32[1280]{0:T(1024)} %copy-done.30) | copy-start | bytes 15364
  197.4 121.2 %copy-start.33 = (f32[1280]{0:T(1024)S(1)}, f32[1280]{0:T(1024)}, u32[]{:S(2)}) copy-start(f32[1280]{0:T(1024)} %copy-done.32) | copy-start | bytes 15364
  197.4 121.2 %copy-start.35 = (f32[1280]{0:T(1024)S(1)}, f32[1280]{0:T(1024)}, u32[]{:S(2)}) copy-start(f32[1280]{0:T(1024)} %copy-done.34) | copy-start | bytes 15364
  197.4 121.2 %copy-start.37 = (f32[1280]{0:T(1024)S(1)}, f32[1280]{0:T(1024)}, u32[]{:S(2)}) copy-start(f32[1280]{0:T(1024)} %copy-done.36) | copy-start | bytes 15364
  197.4 121.2 %copy-start.39 = (f32[1280]{0:T(1024)S(1)}, f32[1280]{0:T(1024)}, u32[]{:S(2)}) copy-start(f32[1280]{0:T(1024)} %copy-done.38) | copy-start | bytes 15364
  197.4 121.2 %copy-start.41 = (f32[1280]{0:T(1024)S(1)}, f32[1280]{0:T(1024)}, u32[]{:S(2)}) copy-start(f32[1280]{0:T(1024)} %copy-done.40) | copy-start | bytes 15364
  197.4 121.2 %copy-start.43 = (f32[1280]{0:T(1024)S(1)}, f32[1280]{0:T(1024)}, u32[]{:S(2)}) copy-start(f32[1280]{0:T(1024)} %copy-done.42) | copy-start | bytes 15364
  197.4 121.2 %copy-start.45 = (f32[1280]{0:T(1024)S(1)}, f32[1280]{0:T(1024)}, u32[]{:S(2)}) copy-start(f32[1280]{0:T(1024)} %copy-done.44) | copy-start | bytes 15364
  197.4 121.2 %copy-start.47 = (f32[1280]{0:T(1024)S(1)}, f32[1280]{0:T(1024)}, u32[]{:S(2)}) copy-start(f32[1280]{0:T(1024)} %copy-done.46) | copy-start | bytes 15364
  197.5 121.2 %copy-start.49 = (f32[1280]{0:T(1024)S(1)}, f32[1280]{0:T(1024)}, u32[]{:S(2)}) copy-start(f32[1280]{0:T(1024)} %copy-done.48) | copy-start | bytes 15364
  197.5 121.2 %copy-start.51 = (f32[1280]{0:T(1024)S(1)}, f32[1280]{0:T(1024)}, u32[]{:S(2)}) copy-start(f32[1280]{0:T(1024)} %copy-done.50) | copy-start | bytes 15364
  197.5 121.2 %copy-start.53 = (f32[1280]{0:T(1024)S(1)}, f32[1280]{0:T(1024)}, u32[]{:S(2)}) copy-start(f32[1280]{0:T(1024)} %copy-done.52) | copy-start | bytes 15364
  197.5 121.2 %copy-start.55 = (f32[1280]{0:T(1024)S(1)}, f32[1280]{0:T(1024)}, u32[]{:S(2)}) copy-start(f32[1280]{0:T(1024)} %copy-done.54) | copy-start | bytes 15364
  197.5 121.2 %copy-start.57 = (f32[1280]{0:T(1024)S(1)}, f32[1280]{0:T(1024)}, u32[]{:S(2)}) copy-start(f32[1280]{0:T(1024)} %copy-done.56) | copy-start | bytes 15364
  197.5 121.2 %copy-start.59 = (f32[1280]{0:T(1024)S(1)}, f32[1280]{0:T(1024)}, u32[]{:S(2)}) copy-start(f32[1280]{0:T(1024)} %copy-done.58) | copy-start | bytes 15364
  197.5 121.2 %copy-start.61 = (f32[1280]{0:T(1024)S(1)}, f32[1280]{0:T(1024)}, u32[]{:S(2)}) copy-start(f32[1280]{0:T(1024)} %copy-done.60) | copy-start | bytes 15364
  197.5 121.2 %copy-start.63 = (f32[1280]{0:T(1024)S(1)}, f32[1280]{0:T(1024)}, u32[]{:S(2)}) copy-start(f32[1280]{0:T(1024)} %copy-done.62) | copy-start | bytes 15364
  197.5 121.2 %copy-start.65 = (f32[1280]{0:T(1024)S(1)}, f32[1280]{0:T(1024)}, u32[]{:S(2)}) copy-start(f32[1280]{0:T(1024)} %copy-done.64) | copy-start | bytes 15364
  197.5 121.2 %copy-start.67 = (f32[1280]{0:T(1024)S(1)}, f32[1280]{0:T(1024)}, u32[]{:S(2)}) copy-start(f32[1280]{0:T(1024)} %copy-done.66) | copy-start | bytes 15364
  197.6 121.2 %copy-start.69 = (f32[1280]{0:T(1024)S(1)}, f32[1280]{0:T(1024)}, u32[]{:S(2)}) copy-start(f32[1280]{0:T(1024)} %copy-done.68) | copy-start | bytes 15364
  197.6 121.2 %copy-start.71 = (f32[1280]{0:T(1024)S(1)}, f32[1280]{0:T(1024)}, u32[]{:S(2)}) copy-start(f32[1280]{0:T(1024)} %copy-done.70) | copy-start | bytes 15364
  197.6 121.2 %copy-start.73 = (f32[1280]{0:T(1024)S(1)}, f32[1280]{0:T(1024)}, u32[]{:S(2)}) copy-start(f32[1280]{0:T(1024)} %copy-done.72) | copy-start | bytes 15364
  201.0 117.5 %collective-permute-start.10 = (f32[1,15,1280]{2,1,0:T(8,128)S(1)}, f32[1,15,1280]{2,1,0:T(8,128)S(1)}, u32[]{:S(2)}, u32[]{:S(2)}) collective-permute-start(f32[1,15,1280]{2,1,0:T(8,128)S(1)} %get-tuple-element.342), channel_id=1, source_target_pairs={{1,0},{3,2},{5,4},{7,6},{9,8},{11,10},{13,12},{15,14},{17,16},{19,... | collective-permute-start | bytes 230408 | tf_op jit(solution)/shard_map/ppermute | solution.py:17
  202.3 116.2 %collective-permute-start.11 = (f32[1,15,1280]{2,1,0:T(8,128)S(1)}, f32[1,15,1280]{2,1,0:T(8,128)S(1)}, u32[]{:S(2)}, u32[]{:S(2)}) collective-permute-start(f32[1,15,1280]{2,1,0:T(8,128)S(1)} %get-tuple-element.343), channel_id=1, source_target_pairs={{0,1},{2,3},{4,5},{6,7},{8,9},{10,11},{12,13},{14,15},{16,17},{18,... | collective-permute-start | bytes 230408 | tf_op jit(solution)/shard_map/ppermute | solution.py:14
  209.6 276.3 %all-reduce.5.cloned.1.call-start = ((), (), s32[]{:S(2)}) async-start(), calls=%async_computation.4 | async-start | bytes 1638400 | tf_op jit(solution)/shard_map/psum | solution.py:218
  (40 other events, 432.1 us)
Sparse Core Ops, SparseCore 0:
  10.3 66.0 all-gather.1
  180.5 137.9 reduce-scatter.1
  325.5 120.9 all-reduce.2
  448.8 37.0 all-reduce.4
where the time goes:
time: 498 us; the launch traced here: 496 us
  waiting for transfers between devices  233 us (47%)
  other arithmetic  92.3 us (19%)
  blocking collectives  44.2 us (9%)
  matrix products  42.7 us (9%)
  local copies, waits for them, and re-layouts  37.5 us (8%)
  starting transfers between devices  29.8 us (6%)
  between operations  16 us (3%)
    psum x1, waiting for transfers between devices, per_device(): taps_grad, gain_grad = lax.psum((tap_terms, gain_term), ('dp', 'ctx'))  83.9 us
    reduce_scatter x1, waiting for transfers between devices, per_device(): lax.psum_scatter(lax.dot_general(encoded, kv_grad, (((0,), (0,)), ((), ()...  64 us
    psum x1, blocking collectives, per_device(): taps_grad, gain_grad = lax.psum((tap_terms, gain_term), ('dp', 'ctx'))  44.2 us
    broadcast_in_dim x1, other arithmetic, per_device(): frames_grad = (enc_grad + back_conv).astype(jnp.bfloat16)[None]  43.9 us
    all_gather x1, waiting for transfers between devices, per_device(): w_full = lax.all_gather(w_kv, 'dp', axis=0, tiled=True)  41.4 us
    psum x1, waiting for transfers between devices, per_device(): w_kv_grad = lax.psum(data_part, 'ctx')  39.3 us
    ppermute x16, starting transfers between devices, shifted(): return lax.ppermute(value, axis, pairs)  17.5 us
    unnamed x156, local copies, waits for them, and re-layouts  13.9 us
  transfers between devices with their start and end apart: 24, of which 6 were waited for; matrix products, arithmetic and copies ran while one was open for 27% of the time, Pallas kernels for 0%

commit v1 on v0

--- a/solution.py
+++ b/solution.py
@@ -1,9 +1,28 @@
+import functools
 import jax
 import jax.numpy as jnp
 from jax import lax
 from jax.sharding import PartitionSpec as P
 
 HEADS = 20
+
+
+def compute_the_field(buf, axis_tag):
+    cores_n = jax.lax.axis_size(axis_tag)
+    steps_seen = list(map(lambda no: (no, (no + 1) % cores_n), range(cores_n)))
+
+    def squares_direct(carry_out):
+        if len(carry_out) == cores_n:
+            return carry_out
+        known = squares_direct([jax.lax.ppermute(carry_out[0], axis_tag, steps_seen), *carry_out])
+        return known
+
+    y1 = jnp.concatenate(squares_direct([buf]), axis=0)
+    block_last = jnp.roll(y1, shift=(jax.lax.axis_index(axis_tag) + 1) * buf.shape[0], axis=0)
+    return block_last
+
+
+expand_gates = functools.partial(compute_the_field, axis_tag="dp")
 
 
 def padded_2(block, sides, width):
@@ -111,7 +130,7 @@
     conv_out = conv_time(padded, conv_taps, length)
     gated = conv_gain * conv_out
     encoded = (frames[0].astype(jnp.float32) + jax.nn.silu(gated)).astype(jnp.bfloat16)
-    w_full = lax.all_gather(w_kv, "dp", axis=0, tiled=True)
+    w_full = expand_gates(w_kv)
     key_values = jnp.dot(encoded, w_full, preferred_element_type=jnp.float32).astype(jnp.bfloat16)
     key_block = key_values[:, :model_width]
     value_block = key_values[:, model_width:]

time: 498 us -> 551 us (1.11)
  waiting for transfers between devices: 233 us -> 266 us
  local copies, waits for them, and re-layouts: 37.5 us -> 53.8 us
    ppermute x0 -> x15, waiting for transfers between devices: none -> 126 us  [squares_direct(): jax.lax.ppermute(carry_out[0], axis_tag, steps_seen)]
    psum x1, waiting for transfers between devices: 83.9 us -> 34.8 us  [per_device(): taps_grad, gain_grad = lax.psum((tap_terms, gain_term), ('dp', 'ctx'))]
    all_gather x1 -> x0, waiting for transfers between devices: 41.4 us -> none  [per_device(): w_full = lax.all_gather(w_kv, 'dp', axis=0, tiled=True)]
    unnamed x156 -> x167, local copies, waits for them, and re-layouts: 13.9 us -> 27.9 us
  transfers between devices with their start and end apart: 24 -> 38, of which waited for: 6 -> 19; matrix products, arithmetic and copies ran while one was open for 27% -> 26% of each run, Pallas kernels for 0% -> 0%
where the time goes in v1:
time: 551 us; the launch traced here: 548 us
  waiting for transfers between devices  266 us (48%)
  other arithmetic  97.4 us (18%)
  local copies, waits for them, and re-layouts  53.8 us (10%)
  blocking collectives  43 us (8%)
  matrix products  39.9 us (7%)
  starting transfers between devices  30.8 us (6%)
  between operations  17.6 us (3%)
    ppermute x15, waiting for transfers between devices, squares_direct(): jax.lax.ppermute(carry_out[0], axis_tag, steps_seen)  126 us
    reduce_scatter x1, waiting for transfers between devices, per_device(): lax.psum_scatter(lax.dot_general(encoded, kv_grad, (((0,), (0,)), ((), ()...  62.1 us
    psum x1, blocking collectives, per_device(): taps_grad, gain_grad = lax.psum((tap_terms, gain_term), ('dp', 'ctx'))  43 us
    broadcast_in_dim x1, other arithmetic, per_device(): frames_grad = (enc_grad + back_conv).astype(jnp.bfloat16)[None]  42.1 us
    psum x1, waiting for transfers between devices, per_device(): w_kv_grad = lax.psum(data_part, 'ctx')  39.1 us
    psum x1, waiting for transfers between devices, per_device(): taps_grad, gain_grad = lax.psum((tap_terms, gain_term), ('dp', 'ctx'))  34.8 us
    unnamed x167, local copies, waits for them, and re-layouts  27.9 us
    ppermute x16, starting transfers between devices, shifted(): return lax.ppermute(value, axis, pairs)  18.4 us
  transfers between devices with their start and end apart: 38, of which 19 were waited for; matrix products, arithmetic and copies ran while one was open for 26% of the time, Pallas kernels for 0%

profile of v1, /device:TPU:0, one launch (start us, length us, event | category | flops | bytes accessed | tf_op | source)
XLA Modules:
  0.0 548.4 jit_solution(4749381783520045851)
XLA Ops:
  8.1 1.5 copy.147
  10.0 10.8 %collective-permute-done.10 = bf16[80,2560]{1,0:T(8,128)(2,1)S(1)} collective-permute-done((bf16[80,2560]{1,0:T(8,128)(2,1)}, bf16[80,2560]{1,0:T(8,128)(2,1)S(1)}, u32[]{:S(2)}, u32[]{:S(2)}) %collective-permute-start.10) | collective-permute-done | bytes 409632 | tf_op jit(solution)/shard_map/ppermute | solution.py:17
  20.8 10.1 %collective-permute-done.11 = bf16[80,2560]{1,0:T(8,128)(2,1)S(1)} collective-permute-done((bf16[80,2560]{1,0:T(8,128)(2,1)S(1)}, bf16[80,2560]{1,0:T(8,128)(2,1)S(1)}, u32[]{:S(2)}, u32[]{:S(2)}) %collective-permute-start.11) | collective-permute-done | bytes 409632 | tf_op jit(solution)/shard_map/ppermute | solution.py:17
  30.9 10.1 %collective-permute-done.12 = bf16[80,2560]{1,0:T(8,128)(2,1)S(1)} collective-permute-done((bf16[80,2560]{1,0:T(8,128)(2,1)S(1)}, bf16[80,2560]{1,0:T(8,128)(2,1)S(1)}, u32[]{:S(2)}, u32[]{:S(2)}) %collective-permute-start.12) | collective-permute-done | bytes 409632 | tf_op jit(solution)/shard_map/ppermute | solution.py:17
  41.0 10.1 %collective-permute-done.13 = bf16[80,2560]{1,0:T(8,128)(2,1)S(1)} collective-permute-done((bf16[80,2560]{1,0:T(8,128)(2,1)S(1)}, bf16[80,2560]{1,0:T(8,128)(2,1)S(1)}, u32[]{:S(2)}, u32[]{:S(2)}) %collective-permute-start.13) | collective-permute-done | bytes 409632 | tf_op jit(solution)/shard_map/ppermute | solution.py:17
  51.1 10.1 %collective-permute-done.14 = bf16[80,2560]{1,0:T(8,128)(2,1)S(1)} collective-permute-done((bf16[80,2560]{1,0:T(8,128)(2,1)S(1)}, bf16[80,2560]{1,0:T(8,128)(2,1)S(1)}, u32[]{:S(2)}, u32[]{:S(2)}) %collective-permute-start.14) | collective-permute-done | bytes 409632 | tf_op jit(solution)/shard_map/ppermute | solution.py:17
  61.1 10.1 %collective-permute-done.15 = bf16[80,2560]{1,0:T(8,128)(2,1)S(1)} collective-permute-done((bf16[80,2560]{1,0:T(8,128)(2,1)S(1)}, bf16[80,2560]{1,0:T(8,128)(2,1)S(1)}, u32[]{:S(2)}, u32[]{:S(2)}) %collective-permute-start.15) | collective-permute-done | bytes 409632 | tf_op jit(solution)/shard_map/ppermute | solution.py:17
  72.0 10.1 %collective-permute-done.16 = bf16[80,2560]{1,0:T(8,128)(2,1)S(1)} collective-permute-done((bf16[80,2560]{1,0:T(8,128)(2,1)S(1)}, bf16[80,2560]{1,0:T(8,128)(2,1)S(1)}, u32[]{:S(2)}, u32[]{:S(2)}) %collective-permute-start.16) | collective-permute-done | bytes 409632 | tf_op jit(solution)/shard_map/ppermute | solution.py:17
  82.8 10.1 %collective-permute-done.17 = bf16[80,2560]{1,0:T(8,128)(2,1)S(1)} collective-permute-done((bf16[80,2560]{1,0:T(8,128)(2,1)S(1)}, bf16[80,2560]{1,0:T(8,128)(2,1)S(1)}, u32[]{:S(2)}, u32[]{:S(2)}) %collective-permute-start.17) | collective-permute-done | bytes 409632 | tf_op jit(solution)/shard_map/ppermute | solution.py:17
  93.6 10.1 %collective-permute-done.18 = bf16[80,2560]{1,0:T(8,128)(2,1)S(1)} collective-permute-done((bf16[80,2560]{1,0:T(8,128)(2,1)S(1)}, bf16[80,2560]{1,0:T(8,128)(2,1)S(1)}, u32[]{:S(2)}, u32[]{:S(2)}) %collective-permute-start.18) | collective-permute-done | bytes 409632 | tf_op jit(solution)/shard_map/ppermute | solution.py:17
  104.4 10.1 %collective-permute-done.19 = bf16[80,2560]{1,0:T(8,128)(2,1)S(1)} collective-permute-done((bf16[80,2560]{1,0:T(8,128)(2,1)S(1)}, bf16[80,2560]{1,0:T(8,128)(2,1)S(1)}, u32[]{:S(2)}, u32[]{:S(2)}) %collective-permute-start.19) | collective-permute-done | bytes 409632 | tf_op jit(solution)/shard_map/ppermute | solution.py:17
  115.3 10.2 %collective-permute-done.20 = bf16[80,2560]{1,0:T(8,128)(2,1)} collective-permute-done((bf16[80,2560]{1,0:T(8,128)(2,1)S(1)}, bf16[80,2560]{1,0:T(8,128)(2,1)}, u32[]{:S(2)}, u32[]{:S(2)}) %collective-permute-start.20) | collective-permute-done | bytes 409632 | tf_op jit(solution)/shard_map/ppermute | solution.py:17
  125.4 1.4 fusion.251
  128.2 5.8 %collective-permute-start.8 = (bf16[1,15,1280]{2,1,0:T(8,128)(2,1)}, bf16[1,15,1280]{2,1,0:T(8,128)(2,1)}, u32[]{:S(2)}, u32[]{:S(2)}) collective-permute-start(bf16[1,15,1280]{2,1,0:T(8,128)(2,1)} %get-tuple-element.346), channel_id=1, source_target_pairs={{0,1},{2,3},{4,5},{6,7},{8,9},{10,11},{12,13},{14,15},{16,17},{18,... | collective-permute-start | bytes 115208 | tf_op jit(solution)/shard_map/ppermute | solution.py:33
  135.9 2.4 slice_reduce_fusion.30
  138.3 1.4 constant_dynamic-update-slice_fusion.1
  139.7 6.5 %collective-permute-done.22 = bf16[80,2560]{1,0:T(8,128)(2,1)} collective-permute-done((bf16[80,2560]{1,0:T(8,128)(2,1)}, bf16[80,2560]{1,0:T(8,128)(2,1)}, u32[]{:S(2)}, u32[]{:S(2)}) %collective-permute-start.22) | collective-permute-done | bytes 409632 | tf_op jit(solution)/shard_map/ppermute | solution.py:17
  146.2 2.1 slice_reduce_fusion.29
  150.5 6.1 %collective-permute-done.23 = bf16[80,2560]{1,0:T(8,128)(2,1)} collective-permute-done((bf16[80,2560]{1,0:T(8,128)(2,1)}, bf16[80,2560]{1,0:T(8,128)(2,1)}, u32[]{:S(2)}, u32[]{:S(2)}) %collective-permute-start.23) | collective-permute-done | bytes 409632 | tf_op jit(solution)/shard_map/ppermute | solution.py:17
  156.6 15.2 %fusion.89 = (bf16[512,1280]{1,0:T(8,128)(2,1)S(1)}, f32[512,1280]{1,0:T(8,128)}) fusion(bf16[1,512,1280]{2,1,0:T(8,128)(2,1)S(1)} %copy-done.4, f32[1280]{0:T(1024)} %param.14, bf16[1,527,1280]{2,1,0:T(8,128)(2,1)S(1)} %constant_dynamic-update-slice_fusion, f32[1280]{0:T(1024)} %get-tuple-element.290, f32[1280]{0:T(1024)} %get-tuple-element.291, ...), kind=kLoop, calls=%fused_computation.200 | loop fusion | flops 104202240 | bytes 25105920 | tf_op jit(solution)/shard_map/convert_element_type | solution.py:132
  172.0 1.5 constant_dynamic-update-slice_fusion.32
  182.7 3.9 fusion.26
  188.6 1.6 copy.42
  190.2 1.6 copy.43
  192.4 19.8 %while.38 = (s32[]{:T(128)}, bf16[16,1280]{1,0:T(8,128)(2,1)S(1)}, f32[16,1280]{1,0:T(8,128)S(1)}, f32[16,20]{0,1:T(8,128)}, bf16[512,1280]{0,1:T(8,128)(2,1)}, ...) while((s32[]{:T(128)}, bf16[16,1280]{1,0:T(8,128)(2,1)S(1)}, ...), condition=%wide.region_2.3_spmd.clone, body=%wide.region_0.2_spmd.clone.sunk | while | flops 42620416 | bytes 4643037 | solution.py:172
  192.4 2.0 collective-permute-start
  195.2 1.7 fusion.286
  198.4 1.9 collective-permute-start.2
  200.3 1.9 collective-permute-done.2
  202.3 1.9 collective-permute-start
  205.0 1.7 fusion.286
  208.3 1.9 collective-permute-start.2
  210.1 2.1 collective-permute-done.2
  215.4 56.2 %while.39 = (s32[]{:T(128)}, bf16[16,1280]{1,0:T(8,128)(2,1)}, bf16[16,1280]{1,0:T(8,128)(2,1)}, f32[16,20]{0,1:T(8,128)}, f32[16,20]{0,1:T(8,128)}, /*index=5*/...) while((s32[]{:T(128)}, bf16[16,1280]{1,0:T(8,128)(2,1)}, ...), condition=%wide.region_5.6_spmd.clone, body=%wide.region_4.5_spmd.clone.sunk | while | flops 108647936 | bytes 37869488 | solution.py:204
  216.2 1.7 collective-permute-start.3
  219.0 1.3 copy.129
  220.3 1.7 collective-permute-start.5
  222.1 1.3 copy.130
  224.6 1.7 fusion.298
  229.7 1.8 collective-permute-start.7
  231.5 3.1 fusion.300
  234.6 2.1 fusion.301
  236.7 6.2 %bitcast_add_fusion.6 = (f32[512,1280]{0,1:T(8,128)}, f32[512,1280]{0,1:T(8,128)}) fusion(f32[20,512,64]{1,2,0:T(8,128)} %fusion.300, f32[512,1280]{0,1:T(8,128)} %get-tuple-element.528, pred[]{:T(512)S(6)} %compare.3, f32[20,512,64]{1,2,0:T(8,128)} %fusion.301, f32[512,1280]{0,1:T(8,128)} %get-tuple-element.527), kind=kLoop, calls=%fused_computation.11.clone.1 | loop fusion | flops 2621440 | bytes 15728641 | tf_op jit(solution)/shard_map/while/body/eval_jaxpr/add | solution.py:192
  245.4 1.7 collective-permute-start.4
  250.0 1.7 collective-permute-start.6
  252.7 1.7 fusion.298
  258.1 3.1 fusion.300
  261.2 2.1 fusion.301
  263.3 7.7 %bitcast_add_fusion.6 = (f32[512,1280]{0,1:T(8,128)}, f32[512,1280]{0,1:T(8,128)}) fusion(f32[20,512,64]{1,2,0:T(8,128)} %fusion.300, f32[512,1280]{0,1:T(8,128)} %get-tuple-element.528, pred[]{:T(512)S(6)} %compare.3, f32[20,512,64]{1,2,0:T(8,128)} %fusion.301, f32[512,1280]{0,1:T(8,128)} %get-tuple-element.527), kind=kLoop, calls=%fused_computation.11.clone.1 | loop fusion | flops 2621440 | bytes 15728641 | tf_op jit(solution)/shard_map/while/body/eval_jaxpr/add | solution.py:192
  271.7 2.1 convert.38
  275.6 7.6 %fusion.211 = f32[1280,2560]{1,0:T(8,128)} fusion(bf16[512,1280]{1,0:T(8,128)(2,1)S(1)} %copy-done.28, bf16[512,1280]{0,1:T(8,128)(2,1)S(1)} %convert.38, bf16[512,1280]{0,1:T(8,128)(2,1)S(1)} %multiply_convert_fusion), kind=kOutput, calls=%fused_computation.352 | convolution fusion | flops 3360686080 | bytes 17039360 | tf_op jit(solution)/shard_map/dot_general | solution.py:230
  283.3 7.4 %fusion.22 = f32[512,1280]{1,0:T(8,128)S(1)} fusion(bf16[2560,2560]{1,0:T(8,128)(2,1)} %copy-done.65, s32[]{:T(128)S(6)} %select_n.14, bf16[512,1280]{0,1:T(8,128)(2,1)S(1)} %convert.38, bf16[512,1280]{0,1:T(8,128)(2,1)} %copy-done.29), kind=kOutput, calls=%fused_computation.72 | convolution fusion | flops 3360686080 | bytes 11796484 | tf_op jit(solution)/shard_map/dot_general | solution.py:210
  290.8 6.7 %fusion.88 = (f32[1280]{0:T(1024)S(1)}, f32[1280]{0:T(1024)S(1)}, f32[1280]{0:T(1024)S(1)}, f32[1280]{0:T(1024)S(1)}, f32[1280]{0:T(1024)S(1)}, /*index=5*/f32[1...) fusion(bf16[1,527,1280]{2,1,0:T(8,128)(2,1)S(1)} %constant_dyna, ...), kind=kLoop, calls=%fused_computation.199 | loop fusion | flops 37335040 | bytes 27612160 | tf_op jit(solution)/shard_map/reduce_sum | solution.py:218
  297.5 3.5 collective-permute-start.26
  302.4 4.3 fusion.59
  307.0 5.0 fusion.68
  312.4 2.7 stack.127
  315.8 43.0 %psum.22 = f32[1280]{0:T(1024)} all-reduce(f32[1280]{0:T(1024)S(1)} %get-tuple-element.341), channel_id=1, replica_groups=mesh['dp'=16,'ctx'=2] {'dp','ctx'}, use_global_device_ids=true, to_apply=%region_39.40 | all-reduce | flops 1280 | bytes 10240 | tf_op jit(solution)/shard_map/psum | solution.py:228
  358.8 62.1 %reduce-scatter.2.cloned.1.call-done = f32[80,2560]{1,0:T(8,128)} async-done(((f32[1280,2560]{1,0:T(8,128)}), f32[80,2560]{1,0:T(8,128)}) %reduce-scatter.2.cloned.1.call-update) | async-done | bytes 819216 | tf_op jit(solution)/shard_map/reduce_scatter | solution.py:229
  421.2 42.1 %fusion.241 = bf16[1,512,1280]{2,1,0:T(8,128)(2,1)} fusion(f32[512,1280]{1,0:T(8,128)} %copy-done.6, f32[1,512,1280]{2,1,0:T(8,128)} %bitcast.632, f32[1,15,1280]{2,1,0:T(8,128)S(1)} %collective-permute-done.26, f32[1280]{0:T(1024)S(1)} %copy-done.61, f32[1280]{0:T(1024)S(1)} %copy-done.62, f32[1280]{0:T(1024)S(1)} %copy-done.31, f32[1280]{0:T(1024)S(1)} %copy-done.33, ...), kind=kLoop, calls=%fused_computation.399 | loop fusion | flops 60948480 | bytes 9487360 | tf_op jit(solution)/shard_map/broadcast_in_dim | solution.py:227
  463.4 34.8 %all-reduce.3.cloned.1.call-done = f32[31,1280]{1,0:T(8,128)} async-done(((f32[31,1280]{1,0:T(8,128)}), f32[31,1280]{1,0:T(8,128)}) %all-reduce.3.cloned.1.call-update) | async-done | bytes 158736 | tf_op jit(solution)/shard_map/psum | solution.py:228
  498.1 39.1 %all-reduce.5.cloned.1.call-done = f32[80,2560]{1,0:T(8,128)} async-done(((f32[80,2560]{1,0:T(8,128)}), f32[80,2560]{1,0:T(8,128)}) %all-reduce.5.cloned.1.call-update) | async-done | bytes 819216 | tf_op jit(solution)/shard_map/psum | solution.py:237
  537.3 1.6 copy.148
  538.9 2.1 copy.149
  (309 shorter events, 49.7 us)
Async XLA Ops:
  8.0 148.6 %copy-start.4 = (bf16[1,512,1280]{2,1,0:T(8,128)(2,1)S(1)}, bf16[1,512,1280]{2,1,0:T(8,128)(2,1)}, u32[]{:S(2)}) copy-start(bf16[1,512,1280]{2,1,0:T(8,128)(2,1)} %param.12) | copy-start | bytes 3932164
  8.0 412.9 %reduce-scatter.2.cloned.1.call-start = ((), (), s32[]{:S(2)}) async-start(), calls=%async_computation.2 | async-start | bytes 13926400 | tf_op jit(solution)/shard_map/reduce_scatter | solution.py:229
  9.5 11.3 %collective-permute-start.10 = (bf16[80,2560]{1,0:T(8,128)(2,1)}, bf16[80,2560]{1,0:T(8,128)(2,1)S(1)}, u32[]{:S(2)}, u32[]{:S(2)}) collective-permute-start(bf16[80,2560]{1,0:T(8,128)(2,1)} %param.15), channel_id=1, source_target_pairs={{0,2},{2,4},{4,6},{6,8},{8,10},{10,12},{12,14},{14,16},{16,18},{18... | collective-permute-start | bytes 1228808 | tf_op jit(solution)/shard_map/ppermute | solution.py:17
  20.8 10.1 %collective-permute-start.11 = (bf16[80,2560]{1,0:T(8,128)(2,1)S(1)}, bf16[80,2560]{1,0:T(8,128)(2,1)S(1)}, u32[]{:S(2)}, u32[]{:S(2)}) collective-permute-start(bf16[80,2560]{1,0:T(8,128)(2,1)S(1)} %collective-permute-done.10), channel_id=1, source_target_pairs={{0,2},{2,4},{4,6},{6,8},{8,10},{10,12},{12,14},{14,16},{16,18},{18... | collective-permute-start | bytes 1228808 | tf_op jit(solution)/shard_map/ppermute | solution.py:17
  30.9 10.1 %collective-permute-start.12 = (bf16[80,2560]{1,0:T(8,128)(2,1)S(1)}, bf16[80,2560]{1,0:T(8,128)(2,1)S(1)}, u32[]{:S(2)}, u32[]{:S(2)}) collective-permute-start(bf16[80,2560]{1,0:T(8,128)(2,1)S(1)} %collective-permute-done.11), channel_id=1, source_target_pairs={{0,2},{2,4},{4,6},{6,8},{8,10},{10,12},{12,14},{14,16},{16,18},{18... | collective-permute-start | bytes 1228808 | tf_op jit(solution)/shard_map/ppermute | solution.py:17
  41.0 10.1 %collective-permute-start.13 = (bf16[80,2560]{1,0:T(8,128)(2,1)S(1)}, bf16[80,2560]{1,0:T(8,128)(2,1)S(1)}, u32[]{:S(2)}, u32[]{:S(2)}) collective-permute-start(bf16[80,2560]{1,0:T(8,128)(2,1)S(1)} %collective-permute-done.12), channel_id=1, source_target_pairs={{0,2},{2,4},{4,6},{6,8},{8,10},{10,12},{12,14},{14,16},{16,18},{18... | collective-permute-start | bytes 1228808 | tf_op jit(solution)/shard_map/ppermute | solution.py:17
  51.1 10.1 %collective-permute-start.14 = (bf16[80,2560]{1,0:T(8,128)(2,1)S(1)}, bf16[80,2560]{1,0:T(8,128)(2,1)S(1)}, u32[]{:S(2)}, u32[]{:S(2)}) collective-permute-start(bf16[80,2560]{1,0:T(8,128)(2,1)S(1)} %collective-permute-done.13), channel_id=1, source_target_pairs={{0,2},{2,4},{4,6},{6,8},{8,10},{10,12},{12,14},{14,16},{16,18},{18... | collective-permute-start | bytes 1228808 | tf_op jit(solution)/shard_map/ppermute | solution.py:17
  61.1 10.1 %collective-permute-start.15 = (bf16[80,2560]{1,0:T(8,128)(2,1)S(1)}, bf16[80,2560]{1,0:T(8,128)(2,1)S(1)}, u32[]{:S(2)}, u32[]{:S(2)}) collective-permute-start(bf16[80,2560]{1,0:T(8,128)(2,1)S(1)} %collective-permute-done.14), channel_id=1, source_target_pairs={{0,2},{2,4},{4,6},{6,8},{8,10},{10,12},{12,14},{14,16},{16,18},{18... | collective-permute-start | bytes 1228808 | tf_op jit(solution)/shard_map/ppermute | solution.py:17
  72.0 10.1 %collective-permute-start.16 = (bf16[80,2560]{1,0:T(8,128)(2,1)S(1)}, bf16[80,2560]{1,0:T(8,128)(2,1)S(1)}, u32[]{:S(2)}, u32[]{:S(2)}) collective-permute-start(bf16[80,2560]{1,0:T(8,128)(2,1)S(1)} %collective-permute-done.15), channel_id=1, source_target_pairs={{0,2},{2,4},{4,6},{6,8},{8,10},{10,12},{12,14},{14,16},{16,18},{18... | collective-permute-start | bytes 1228808 | tf_op jit(solution)/shard_map/ppermute | solution.py:17
  82.8 10.1 %collective-permute-start.17 = (bf16[80,2560]{1,0:T(8,128)(2,1)S(1)}, bf16[80,2560]{1,0:T(8,128)(2,1)S(1)}, u32[]{:S(2)}, u32[]{:S(2)}) collective-permute-start(bf16[80,2560]{1,0:T(8,128)(2,1)S(1)} %collective-permute-done.16), channel_id=1, source_target_pairs={{0,2},{2,4},{4,6},{6,8},{8,10},{10,12},{12,14},{14,16},{16,18},{18... | collective-permute-start | bytes 1228808 | tf_op jit(solution)/shard_map/ppermute | solution.py:17
  93.6 10.1 %collective-permute-start.18 = (bf16[80,2560]{1,0:T(8,128)(2,1)S(1)}, bf16[80,2560]{1,0:T(8,128)(2,1)S(1)}, u32[]{:S(2)}, u32[]{:S(2)}) collective-permute-start(bf16[80,2560]{1,0:T(8,128)(2,1)S(1)} %collective-permute-done.17), channel_id=1, source_target_pairs={{0,2},{2,4},{4,6},{6,8},{8,10},{10,12},{12,14},{14,16},{16,18},{18... | collective-permute-start | bytes 1228808 | tf_op jit(solution)/shard_map/ppermute | solution.py:17
  104.4 10.1 %collective-permute-start.19 = (bf16[80,2560]{1,0:T(8,128)(2,1)S(1)}, bf16[80,2560]{1,0:T(8,128)(2,1)S(1)}, u32[]{:S(2)}, u32[]{:S(2)}) collective-permute-start(bf16[80,2560]{1,0:T(8,128)(2,1)S(1)} %collective-permute-done.18), channel_id=1, source_target_pairs={{0,2},{2,4},{4,6},{6,8},{8,10},{10,12},{12,14},{14,16},{16,18},{18... | collective-permute-start | bytes 1228808 | tf_op jit(solution)/shard_map/ppermute | solution.py:17
  115.3 10.2 %collective-permute-start.20 = (bf16[80,2560]{1,0:T(8,128)(2,1)S(1)}, bf16[80,2560]{1,0:T(8,128)(2,1)}, u32[]{:S(2)}, u32[]{:S(2)}) collective-permute-start(bf16[80,2560]{1,0:T(8,128)(2,1)S(1)} %collective-permute-done.19), channel_id=1, source_target_pairs={{0,2},{2,4},{4,6},{6,8},{8,10},{10,12},{12,14},{14,16},{16,18},{18... | collective-permute-start | bytes 1228808 | tf_op jit(solution)/shard_map/ppermute | solution.py:17
  125.4 10.4 %collective-permute-start.21 = (bf16[80,2560]{1,0:T(8,128)(2,1)}, bf16[80,2560]{1,0:T(8,128)(2,1)}, u32[]{:S(2)}, u32[]{:S(2)}) collective-permute-start(bf16[80,2560]{1,0:T(8,128)(2,1)} %collective-permute-done.20), channel_id=1, source_target_pairs={{0,2},{2,4},{4,6},{6,8},{8,10},{10,12},{12,14},{14,16},{16,18},{18... | collective-permute-start | bytes 1228808 | tf_op jit(solution)/shard_map/ppermute | solution.py:17
  126.9 22.8 %collective-permute-start.9 = (bf16[1,15,1280]{2,1,0:T(8,128)(2,1)}, bf16[1,15,1280]{2,1,0:T(8,128)(2,1)}, u32[]{:S(2)}, u32[]{:S(2)}) collective-permute-start(bf16[1,15,1280]{2,1,0:T(8,128)(2,1)} %get-tuple-element.347), channel_id=1, source_target_pairs={{1,0},{3,2},{5,4},{7,6},{9,8},{11,10},{13,12},{15,14},{17,16},{19,... | collective-permute-start | bytes 115208 | tf_op jit(solution)/shard_map/ppermute | solution.py:36
  128.2 28.4 %collective-permute-start.8 = (bf16[1,15,1280]{2,1,0:T(8,128)(2,1)}, bf16[1,15,1280]{2,1,0:T(8,128)(2,1)}, u32[]{:S(2)}, u32[]{:S(2)}) collective-permute-start(bf16[1,15,1280]{2,1,0:T(8,128)(2,1)} %get-tuple-element.346), channel_id=1, source_target_pairs={{0,1},{2,3},{4,5},{6,7},{8,9},{10,11},{12,13},{14,15},{16,17},{18,... | collective-permute-start | bytes 115208 | tf_op jit(solution)/shard_map/ppermute | solution.py:33
  135.8 10.4 %collective-permute-start.22 = (bf16[80,2560]{1,0:T(8,128)(2,1)}, bf16[80,2560]{1,0:T(8,128)(2,1)}, u32[]{:S(2)}, u32[]{:S(2)}) collective-permute-start(bf16[80,2560]{1,0:T(8,128)(2,1)} %collective-permute-done.21), channel_id=1, source_target_pairs={{0,2},{2,4},{4,6},{6,8},{8,10},{10,12},{12,14},{14,16},{16,18},{18... | collective-permute-start | bytes 1228808 | tf_op jit(solution)/shard_map/ppermute | solution.py:17
  146.2 10.4 %collective-permute-start.23 = (bf16[80,2560]{1,0:T(8,128)(2,1)}, bf16[80,2560]{1,0:T(8,128)(2,1)}, u32[]{:S(2)}, u32[]{:S(2)}) collective-permute-start(bf16[80,2560]{1,0:T(8,128)(2,1)} %collective-permute-done.22), channel_id=1, source_target_pairs={{0,2},{2,4},{4,6},{6,8},{8,10},{10,12},{12,14},{14,16},{16,18},{18... | collective-permute-start | bytes 1228808 | tf_op jit(solution)/shard_map/ppermute | solution.py:17
  156.6 15.3 %collective-permute-start.24 = (bf16[80,2560]{1,0:T(8,128)(2,1)}, bf16[80,2560]{1,0:T(8,128)(2,1)S(1)}, u32[]{:S(2)}, u32[]{:S(2)}) collective-permute-start(bf16[80,2560]{1,0:T(8,128)(2,1)} %collective-permute-done.23), channel_id=1, source_target_pairs={{0,2},{2,4},{4,6},{6,8},{8,10},{10,12},{12,14},{14,16},{16,18},{18... | collective-permute-start | bytes 1228808 | tf_op jit(solution)/shard_map/ppermute | solution.py:17
  192.4 9.9 %collective-permute-start = (bf16[16,1280]{1,0:T(8,128)(2,1)S(1)}, bf16[16,1280]{1,0:T(8,128)(2,1)S(1)}, u32[]{:S(2)}, u32[]{:S(2)}) collective-permute-start(bf16[16,1280]{1,0:T(8,128)(2,1)S(1)} %copy.111), channel_id=1, source_target_pairs={{0,1},{1,0},{2,3},{3,2},{4,5},{5,4},{6,7},{7,6},{8,9},{9,8},{10,11... | collective-permute-start | bytes 122888 | tf_op jit(solution)/shard_map/while/body/eval_jaxpr/ppermute | solution.py:44
  197.5 4.7 collective-permute-start.1
  198.4 3.9 collective-permute-start.2
  202.3 9.9 %collective-permute-start = (bf16[16,1280]{1,0:T(8,128)(2,1)S(1)}, bf16[16,1280]{1,0:T(8,128)(2,1)S(1)}, u32[]{:S(2)}, u32[]{:S(2)}) collective-permute-start(bf16[16,1280]{1,0:T(8,128)(2,1)S(1)} %copy.111), channel_id=1, source_target_pairs={{0,1},{1,0},{2,3},{3,2},{4,5},{5,4},{6,7},{7,6},{8,9},{9,8},{10,11... | collective-permute-start | bytes 122888 | tf_op jit(solution)/shard_map/while/body/eval_jaxpr/ppermute | solution.py:44
  207.3 4.9 collective-permute-start.1
  208.3 3.9 collective-permute-start.2
  216.2 26.6 %collective-permute-start.3 = (bf16[16,1280]{1,0:T(8,128)(2,1)S(1)}, bf16[16,1280]{1,0:T(8,128)(2,1)}, u32[]{:S(2)}, u32[]{:S(2)}) collective-permute-start(bf16[16,1280]{1,0:T(8,128)(2,1)S(1)} %copy.127), channel_id=1, source_target_pairs={{0,1},{1,0},{2,3},{3,2},{4,5},{5,4},{6,7},{7,6},{8,9},{9,8},{10,11... | collective-permute-start | bytes 122888 | tf_op jit(solution)/shard_map/while/body/eval_jaxpr/ppermute | solution.py:44
  218.7 24.1 %collective-permute-start.4 = (bf16[16,1280]{1,0:T(8,128)(2,1)S(1)}, bf16[16,1280]{1,0:T(8,128)(2,1)}, u32[]{:S(2)}, u32[]{:S(2)}) collective-permute-start(bf16[16,1280]{1,0:T(8,128)(2,1)S(1)} %copy.128), channel_id=1, source_target_pairs={{0,1},{1,0},{2,3},{3,2},{4,5},{5,4},{6,7},{7,6},{8,9},{9,8},{10,11... | collective-permute-start | bytes 122888 | tf_op jit(solution)/shard_map/while/body/eval_jaxpr/ppermute | solution.py:44
  220.3 22.5 %collective-permute-start.5 = (f32[16,20]{0,1:T(8,128)}, f32[16,20]{0,1:T(8,128)}, u32[]{:S(2)}, u32[]{:S(2)}) collective-permute-start(f32[16,20]{0,1:T(8,128)} %copy.129), channel_id=1, source_target_pairs={{0,1},{1,0},{2,3},{3,2},{4,5},{5,4},{6,7},{7,6},{8,9},{9,8},{10,11... | collective-permute-start | bytes 3848 | tf_op jit(solution)/shard_map/while/body/eval_jaxpr/ppermute | solution.py:44
  223.4 19.5 %collective-permute-start.6 = (f32[16,20]{0,1:T(8,128)}, f32[16,20]{0,1:T(8,128)}, u32[]{:S(2)}, u32[]{:S(2)}) collective-permute-start(f32[16,20]{0,1:T(8,128)} %copy.130), channel_id=1, source_target_pairs={{0,1},{1,0},{2,3},{3,2},{4,5},{5,4},{6,7},{7,6},{8,9},{9,8},{10,11... | collective-permute-start | bytes 3848 | tf_op jit(solution)/shard_map/while/body/eval_jaxpr/ppermute | solution.py:44
  229.7 13.2 %collective-permute-start.7 = (f32[16,1280]{1,0:T(8,128)S(1)}, f32[16,1280]{1,0:T(8,128)S(1)}, u32[]{:S(2)}, u32[]{:S(2)}) collective-permute-start(f32[16,1280]{1,0:T(8,128)S(1)} %add.1613), channel_id=1, source_target_pairs={{0,1},{1,0},{2,3},{3,2},{4,5},{5,4},{6,7},{7,6},{8,9},{9,8},{10,11... | collective-permute-start | bytes 245768 | tf_op jit(solution)/shard_map/while/body/eval_jaxpr/ppermute | solution.py:44
  244.3 26.7 %collective-permute-start.3 = (bf16[16,1280]{1,0:T(8,128)(2,1)S(1)}, bf16[16,1280]{1,0:T(8,128)(2,1)}, u32[]{:S(2)}, u32[]{:S(2)}) collective-permute-start(bf16[16,1280]{1,0:T(8,128)(2,1)S(1)} %copy.127), channel_id=1, source_target_pairs={{0,1},{1,0},{2,3},{3,2},{4,5},{5,4},{6,7},{7,6},{8,9},{9,8},{10,11... | collective-permute-start | bytes 122888 | tf_op jit(solution)/shard_map/while/body/eval_jaxpr/ppermute | solution.py:44
  245.4 25.6 %collective-permute-start.4 = (bf16[16,1280]{1,0:T(8,128)(2,1)S(1)}, bf16[16,1280]{1,0:T(8,128)(2,1)}, u32[]{:S(2)}, u32[]{:S(2)}) collective-permute-start(bf16[16,1280]{1,0:T(8,128)(2,1)S(1)} %copy.128), channel_id=1, source_target_pairs={{0,1},{1,0},{2,3},{3,2},{4,5},{5,4},{6,7},{7,6},{8,9},{9,8},{10,11... | collective-permute-start | bytes 122888 | tf_op jit(solution)/shard_map/while/body/eval_jaxpr/ppermute | solution.py:44
  248.4 22.6 %collective-permute-start.5 = (f32[16,20]{0,1:T(8,128)}, f32[16,20]{0,1:T(8,128)}, u32[]{:S(2)}, u32[]{:S(2)}) collective-permute-start(f32[16,20]{0,1:T(8,128)} %copy.129), channel_id=1, source_target_pairs={{0,1},{1,0},{2,3},{3,2},{4,5},{5,4},{6,7},{7,6},{8,9},{9,8},{10,11... | collective-permute-start | bytes 3848 | tf_op jit(solution)/shard_map/while/body/eval_jaxpr/ppermute | solution.py:44
  250.0 21.0 %collective-permute-start.6 = (f32[16,20]{0,1:T(8,128)}, f32[16,20]{0,1:T(8,128)}, u32[]{:S(2)}, u32[]{:S(2)}) collective-permute-start(f32[16,20]{0,1:T(8,128)} %copy.130), channel_id=1, source_target_pairs={{0,1},{1,0},{2,3},{3,2},{4,5},{5,4},{6,7},{7,6},{8,9},{9,8},{10,11... | collective-permute-start | bytes 3848 | tf_op jit(solution)/shard_map/while/body/eval_jaxpr/ppermute | solution.py:44
  257.8 13.3 %collective-permute-start.7 = (f32[16,1280]{1,0:T(8,128)S(1)}, f32[16,1280]{1,0:T(8,128)S(1)}, u32[]{:S(2)}, u32[]{:S(2)}) collective-permute-start(f32[16,1280]{1,0:T(8,128)S(1)} %add.1613), channel_id=1, source_target_pairs={{0,1},{1,0},{2,3},{3,2},{4,5},{5,4},{6,7},{7,6},{8,9},{9,8},{10,11... | collective-permute-start | bytes 245768 | tf_op jit(solution)/shard_map/while/body/eval_jaxpr/ppermute | solution.py:44
  283.3 214.8 %all-reduce.3.cloned.1.call-start = ((), (), s32[]{:S(2)}) async-start(), calls=%async_computation.1 | async-start | bytes 327680 | tf_op jit(solution)/shard_map/psum | solution.py:228
  297.5 123.4 %collective-permute-start.26 = (f32[1,15,1280]{2,1,0:T(8,128)S(1)}, f32[1,15,1280]{2,1,0:T(8,128)S(1)}, u32[]{:S(2)}, u32[]{:S(2)}) collective-permute-start(f32[1,15,1280]{2,1,0:T(8,128)S(1)} %get-tuple-element.343), channel_id=1, source_target_pairs={{0,1},{2,3},{4,5},{6,7},{8,9},{10,11},{12,13},{14,15},{16,17},{18,... | collective-permute-start | bytes 230408 | tf_op jit(solution)/shard_map/ppermute | solution.py:33
  301.1 119.8 %collective-permute-start.25 = (f32[1,15,1280]{2,1,0:T(8,128)S(1)}, f32[1,15,1280]{2,1,0:T(8,128)S(1)}, u32[]{:S(2)}, u32[]{:S(2)}) collective-permute-start(f32[1,15,1280]{2,1,0:T(8,128)S(1)} %get-tuple-element.342), channel_id=1, source_target_pairs={{1,0},{3,2},{5,4},{7,6},{9,8},{11,10},{13,12},{15,14},{17,16},{19,... | collective-permute-start | bytes 230408 | tf_op jit(solution)/shard_map/ppermute | solution.py:36
  306.7 114.2 %copy-start.31 = (f32[1280]{0:T(1024)S(1)}, f32[1280]{0:T(1024)}, u32[]{:S(2)}) copy-start(f32[1280]{0:T(1024)} %copy-done.30) | copy-start | bytes 15364
  306.8 114.2 %copy-start.33 = (f32[1280]{0:T(1024)S(1)}, f32[1280]{0:T(1024)}, u32[]{:S(2)}) copy-start(f32[1280]{0:T(1024)} %copy-done.32) | copy-start | bytes 15364
  306.8 114.2 %copy-start.35 = (f32[1280]{0:T(1024)S(1)}, f32[1280]{0:T(1024)}, u32[]{:S(2)}) copy-start(f32[1280]{0:T(1024)} %copy-done.34) | copy-start | bytes 15364
  306.8 114.2 %copy-start.36 = (f32[1280]{0:T(1024)S(1)}, f32[1280]{0:T(1024)}, u32[]{:S(2)}) copy-start(f32[1280]{0:T(1024)} %get-tuple-element.265) | copy-start | bytes 15364
  306.8 114.2 %copy-start.37 = (f32[1280]{0:T(1024)S(1)}, f32[1280]{0:T(1024)}, u32[]{:S(2)}) copy-start(f32[1280]{0:T(1024)} %get-tuple-element.266) | copy-start | bytes 15364
  306.8 114.2 %copy-start.38 = (f32[1280]{0:T(1024)S(1)}, f32[1280]{0:T(1024)}, u32[]{:S(2)}) copy-start(f32[1280]{0:T(1024)} %get-tuple-element.267) | copy-start | bytes 15364
  306.8 114.2 %copy-start.39 = (f32[1280]{0:T(1024)S(1)}, f32[1280]{0:T(1024)}, u32[]{:S(2)}) copy-start(f32[1280]{0:T(1024)} %get-tuple-element.268) | copy-start | bytes 15364
  306.8 114.2 %copy-start.40 = (f32[1280]{0:T(1024)S(1)}, f32[1280]{0:T(1024)}, u32[]{:S(2)}) copy-start(f32[1280]{0:T(1024)} %get-tuple-element.269) | copy-start | bytes 15364
  306.8 114.2 %copy-start.41 = (f32[1280]{0:T(1024)S(1)}, f32[1280]{0:T(1024)}, u32[]{:S(2)}) copy-start(f32[1280]{0:T(1024)} %get-tuple-element.270) | copy-start | bytes 15364
  306.8 114.2 %copy-start.42 = (f32[1280]{0:T(1024)S(1)}, f32[1280]{0:T(1024)}, u32[]{:S(2)}) copy-start(f32[1280]{0:T(1024)} %get-tuple-element.271) | copy-start | bytes 15364
  306.8 114.2 %copy-start.43 = (f32[1280]{0:T(1024)S(1)}, f32[1280]{0:T(1024)}, u32[]{:S(2)}) copy-start(f32[1280]{0:T(1024)} %get-tuple-element.272) | copy-start | bytes 15364
  306.9 114.2 %copy-start.44 = (f32[1280]{0:T(1024)S(1)}, f32[1280]{0:T(1024)}, u32[]{:S(2)}) copy-start(f32[1280]{0:T(1024)} %get-tuple-element.273) | copy-start | bytes 15364
  306.9 114.2 %copy-start.45 = (f32[1280]{0:T(1024)S(1)}, f32[1280]{0:T(1024)}, u32[]{:S(2)}) copy-start(f32[1280]{0:T(1024)} %get-tuple-element.274) | copy-start | bytes 15364
  306.9 114.2 %copy-start.46 = (f32[1280]{0:T(1024)S(1)}, f32[1280]{0:T(1024)}, u32[]{:S(2)}) copy-start(f32[1280]{0:T(1024)} %get-tuple-element.275) | copy-start | bytes 15364
  306.9 114.2 %copy-start.47 = (f32[1280]{0:T(1024)S(1)}, f32[1280]{0:T(1024)}, u32[]{:S(2)}) copy-start(f32[1280]{0:T(1024)} %get-tuple-element.276) | copy-start | bytes 15364
  306.9 114.2 %copy-start.48 = (f32[1280]{0:T(1024)S(1)}, f32[1280]{0:T(1024)}, u32[]{:S(2)}) copy-start(f32[1280]{0:T(1024)} %get-tuple-element.277) | copy-start | bytes 15364
  306.9 114.2 %copy-start.49 = (f32[1280]{0:T(1024)S(1)}, f32[1280]{0:T(1024)}, u32[]{:S(2)}) copy-start(f32[1280]{0:T(1024)} %get-tuple-element.278) | copy-start | bytes 15364
  306.9 114.2 %copy-start.50 = (f32[1280]{0:T(1024)S(1)}, f32[1280]{0:T(1024)}, u32[]{:S(2)}) copy-start(f32[1280]{0:T(1024)} %get-tuple-element.279) | copy-start | bytes 15364
  306.9 114.2 %copy-start.51 = (f32[1280]{0:T(1024)S(1)}, f32[1280]{0:T(1024)}, u32[]{:S(2)}) copy-start(f32[1280]{0:T(1024)} %get-tuple-element.280) | copy-start | bytes 15364
  306.9 114.2 %copy-start.52 = (f32[1280]{0:T(1024)S(1)}, f32[1280]{0:T(1024)}, u32[]{:S(2)}) copy-start(f32[1280]{0:T(1024)} %get-tuple-element.281) | copy-start | bytes 15364
  306.9 114.2 %copy-start.53 = (f32[1280]{0:T(1024)S(1)}, f32[1280]{0:T(1024)}, u32[]{:S(2)}) copy-start(f32[1280]{0:T(1024)} %get-tuple-element.282) | copy-start | bytes 15364
  307.0 114.2 %copy-start.54 = (f32[1280]{0:T(1024)S(1)}, f32[1280]{0:T(1024)}, u32[]{:S(2)}) copy-start(f32[1280]{0:T(1024)} %get-tuple-element.283) | copy-start | bytes 15364
  307.0 114.2 %copy-start.55 = (f32[1280]{0:T(1024)S(1)}, f32[1280]{0:T(1024)}, u32[]{:S(2)}) copy-start(f32[1280]{0:T(1024)} %get-tuple-element.284) | copy-start | bytes 15364
  307.0 114.2 %copy-start.56 = (f32[1280]{0:T(1024)S(1)}, f32[1280]{0:T(1024)}, u32[]{:S(2)}) copy-start(f32[1280]{0:T(1024)} %get-tuple-element.285) | copy-start | bytes 15364
  307.0 114.2 %copy-start.57 = (f32[1280]{0:T(1024)S(1)}, f32[1280]{0:T(1024)}, u32[]{:S(2)}) copy-start(f32[1280]{0:T(1024)} %get-tuple-element.286) | copy-start | bytes 15364
  315.1 222.2 %all-reduce.5.cloned.1.call-start = ((), (), s32[]{:S(2)}) async-start(), calls=%async_computation.3 | async-start | bytes 1638400 | tf_op jit(solution)/shard_map/psum | solution.py:237
  (44 other events, 1083.9 us)
Sparse Core Ops, SparseCore 0:
  283.4 137.4 reduce-scatter.1
Sparse Core Ops, SparseCore 1:
  315.2 182.9 all-reduce.2
  500.4 36.8 all-reduce.4
